TPU v7x, 256 devices: a whole 4x4x8 slice. The times are simulated.
256 devices in a mesh: prow: 16 (over x, y), pcol: 16 (over z, core).
Axes of the slice: x: 4, y: 4, z: 8, core: 2. Of those that a mesh axis runs over, the one named last changes fastest.
Arguments:
- known_inverse: bfloat16 [32768, 16, 16, 128], P('prow', None, 'pcol'), may hold values from -6 to 6
- pattern: int32 [256, 16, 16, 1], P('prow', None, 'pcol'), may hold values 0 or 1
- panel_one: bfloat16 [32768, 512], P(('prow', 'pcol')), may hold values from -0.03125 to 0.03125
- panel_two: bfloat16 [32768, 512], P(('prow', 'pcol')), may hold values from -0.03125 to 0.03125
- panel_top: bfloat16 [512, 512], replicated, may hold values from -0.25 to 0.25
- structure: int32 [32768], P(('prow', 'pcol')), may hold values from 0 to 1, as said below
- diag_one: bfloat16 [512, 512], replicated, may hold values from -6 to 6
- diag_two: bfloat16 [512, 512], replicated, may hold values from -6 to 6
Outputs:
- inverse_one: bfloat16 [32768, 512], P(('prow', 'pcol'))
- corner_one: bfloat16 [512, 512], replicated
- inverse_top: bfloat16 [512, 512], replicated
- inverse_two: bfloat16 [32768, 512], P(('prow', 'pcol'))
- corner_two: bfloat16 [512, 512], replicated
Inputs may be any that keep to these rules, and one draw needn't show every extreme that they name: `structure`: in every aligned pair of rows (2 k and 2 k + 1) at least one entry is 1.
All inputs are finite; a program needn't handle non-finite values. No bound on the sum of `pattern` on one device may be relied on, other than what follows from the above.
Results may differ from a plain program's by a relative error of at most 0.0058.
Values may be sent and summed in bfloat16 or wider, within the bound.
A program may use at most 128 MiB of HBM per device.

v0:
```python
import jax
import jax.numpy as jnp
from jax import lax
from jax.sharding import PartitionSpec as P

BLK = 128


def on_device(
    known_inverse, pattern, panel_one, panel_two, panel_top, structure, diag_one, diag_two
):
    row_count = known_inverse.shape[0]
    col_groups = known_inverse.shape[1]
    piece_rows = known_inverse.shape[3]
    block_rows = row_count // BLK
    piece_blocks = piece_rows // BLK
    shaped = known_inverse.reshape(block_rows, BLK, col_groups, piece_blocks, BLK)
    flag_table = pattern.reshape(block_rows, 1, col_groups, piece_blocks, 1)
    masked = jnp.where(flag_table > 0, shaped, jnp.zeros_like(shaped)).reshape(
        row_count, col_groups * piece_rows
    )
    row_flags = structure.reshape(piece_rows, 1) > 0
    masked_two = jnp.where(row_flags, panel_two, jnp.zeros_like(panel_two))

    def accumulate(pieces):
        return jnp.dot(masked, pieces, preferred_element_type=jnp.float32)

    partial_one = accumulate(lax.all_gather(panel_one, "prow", axis=0, tiled=True))
    reduced_one = lax.psum_scatter(partial_one, "pcol", scatter_dimension=0, tiled=True)
    partial_two = accumulate(lax.all_gather(masked_two, "prow", axis=0, tiled=True))
    reduced_two = lax.psum_scatter(partial_two, "pcol", scatter_dimension=0, tiled=True)
    inverse_one = (-reduced_one).astype(jnp.bfloat16)
    own_term = jnp.dot(panel_one.T, inverse_one, preferred_element_type=jnp.float32)
    cross_local = jnp.dot(inverse_one.T, masked_two, preferred_element_type=jnp.float32)
    lower_two = -(reduced_two + jnp.dot(inverse_one, panel_top, preferred_element_type=jnp.float32))
    inverse_two = jnp.where(row_flags, lower_two, jnp.zeros_like(lower_two)).astype(jnp.bfloat16)
    tail_local = jnp.dot(masked_two.T, inverse_two, preferred_element_type=jnp.float32)
    top_weights = panel_top.astype(jnp.float32)
    own_sum, cross_sum = lax.psum((own_term, cross_local), ("prow", "pcol"))
    corner_full = diag_one.astype(jnp.float32) - own_sum
    top_value = jnp.dot(corner_full, top_weights, precision=lax.Precision.HIGHEST) + cross_sum
    inverse_top = (-top_value).astype(jnp.bfloat16)
    tail_sum = lax.psum(tail_local, ("prow", "pcol"))
    corner_two = (
        diag_two.astype(jnp.float32)
        - jnp.dot(panel_top.T, inverse_top, preferred_element_type=jnp.float32)
        - tail_sum
    )
    return (
        inverse_one,
        corner_full.astype(jnp.bfloat16),
        inverse_top,
        inverse_two,
        corner_two.astype(jnp.bfloat16),
    )


def solution(mesh):
    in_specs = (
        P("prow", None, "pcol", None),
        P("prow", None, "pcol", None),
        P(("prow", "pcol"), None),
        P(("prow", "pcol"), None),
        P(),
        P(("prow", "pcol")),
        P(),
        P(),
    )
    out_specs = (P(("prow", "pcol"), None), P(), P(), P(("prow", "pcol"), None), P())
    return jax.shard_map(
        on_device, mesh=mesh, in_specs=in_specs, out_specs=out_specs, check_vma=False
    )
```

profile of v0, /device:TPU:8, one launch (start us, length us, event | category | flops | bytes accessed | tf_op | source)
XLA Modules:
  0.0 526.8 jit_solution(959092906501539637)
XLA Ops:
  7.2 0.0 all-gather.3.cloned.1.call-start
  7.2 0.7 all-gather.3.cloned.1.call-update
  7.9 0.0 all-gather.5.cloned.1.call-start
  8.0 0.7 broadcast_compare_fusion.1
  8.6 1.6 broadcast_select_fusion
  10.3 0.0 all-gather.5.cloned.1.call-update
  10.3 0.0 reduce-scatter.3.cloned.1.call-start
  10.3 0.7 broadcast_compare_fusion
  11.1 51.9 %all-gather.3.cloned.1.call-done = bf16[2048,512]{1,0:T(8,128)(2,1)} async-done(((bf16[128,512]{1,0:T(8,128)(2,1)}), bf16[2048,512]{1,0:T(8,128)(2,1)}) %all-gather.3.cloned.1.call-update) | async-done | bytes 2097168 | tf_op jit(solution)/shard_map/all_gather | solution.py:28
  63.0 1.1 broadcast_in_dim.33
  64.1 2.0 copy-done.1
  66.1 10.0 %fusion.1 = f32[2048,512]{1,0:T(8,128)} fusion(bf16[2048,512]{1,0:T(8,128)(2,1)S(1)} %copy-done.10, pred[256,8,16,128]{3,2,1,0:T(8,128)(4,1)S(1)} %bitcast.40, bf16[256,8,16,128]{3,2,1,0:T(8,128)(2,1)} %bitcast.43), kind=kOutput, calls=%fused_computation.2 | convolution fusion | flops 4299161600 | bytes 18874368 | tf_op jit(solution)/shard_map/dot_general | solution.py:26
  76.1 0.0 reduce-scatter.5.cloned.1.call-start
  76.2 39.2 %all-gather.5.cloned.1.call-done = bf16[2048,512]{1,0:T(8,128)(2,1)} async-done(((bf16[128,512]{1,0:T(8,128)(2,1)}), bf16[2048,512]{1,0:T(8,128)(2,1)}) %all-gather.5.cloned.1.call-update) | async-done | bytes 2097168 | tf_op jit(solution)/shard_map/all_gather | solution.py:30
  115.4 11.7 %fusion = f32[2048,512]{1,0:T(8,128)} fusion(bf16[2048,512]{1,0:T(8,128)(2,1)} %all-gather.5.cloned.1.call-done, pred[256,8,16,128]{3,2,1,0:T(8,128)(4,1)} %bitcast.41, bf16[256,8,16,128]{3,2,1,0:T(8,128)(2,1)} %bitcast.44), kind=kOutput, calls=%fused_computation.1 | convolution fusion | flops 4299161600 | bytes 18874368 | tf_op jit(solution)/shard_map/dot_general | solution.py:26
  127.1 0.0 reduce-scatter.5.cloned.1.call-update
  127.1 0.2 all-reduce.3.cloned.1.call-start
  127.3 53.2 %reduce-scatter.3.cloned.1.call-done = f32[128,512]{1,0:T(8,128)} async-done(((f32[2048,512]{1,0:T(8,128)}), f32[128,512]{1,0:T(8,128)}) %reduce-scatter.3.cloned.1.call-update) | async-done | bytes 262160 | tf_op jit(solution)/shard_map/reduce_scatter | solution.py:29
  180.6 1.0 negate_convert_fusion
  181.6 1.3 fusion.13
  182.9 1.3 convolution_bitcast_fusion.1
  184.2 59.9 %reduce-scatter.5.cloned.1.call-done = f32[128,512]{1,0:T(8,128)} async-done(((f32[2048,512]{1,0:T(8,128)}), f32[128,512]{1,0:T(8,128)}) %reduce-scatter.5.cloned.1.call-update) | async-done | bytes 262160 | tf_op jit(solution)/shard_map/reduce_scatter | solution.py:31
  244.1 1.2 fusion.9
  245.3 1.3 fusion.14
  246.7 0.2 copy.13
  246.9 0.2 copy.14
  247.2 266.5 %all-reduce.3.cloned.1.call-done = (f32[512,512]{0,1:T(8,128)}, f32[512,512]{1,0:T(8,128)}, f32[512,512]{0,1:T(8,128)}) async-done(((f32[512,512]{0,1:T(8,128)}, f32[512,512]{1,0:T(8,128)}, f32[512,512]{0,1:T(8,128)}), (f32[512,512]{0,1:T(8,128)}, f32[512,512]{1,0:T(8,128)}, f32[512,512]{0,1:T(8,128)})) %all-reduce.3.cloned.1.call-update) | async-done | bytes 3145744 | tf_op jit(solution)/shard_map/psum | solution.py:39
  513.7 1.5 fusion.10
  515.1 2.6 fusion.5
  517.7 0.5 fusion.6
  518.2 1.0 copy.17
  519.2 1.0 copy.16
  (24 shorter events, 0.1 us)
Async XLA Ops:
  7.2 237.0 %copy-start = (bf16[512,512]{1,0:T(8,128)(2,1)S(1)}, bf16[512,512]{1,0:T(8,128)(2,1)}, u32[]{:S(2)}) copy-start(bf16[512,512]{1,0:T(8,128)(2,1)} %param.12) | copy-start | bytes 1572868
  7.2 55.8 %all-gather.3.cloned.1.call-start = ((), (), s32[]{:S(2)}) async-start(), calls=%async_computation.2 | async-start | bytes 2228224 | tf_op jit(solution)/shard_map/all_gather | solution.py:28
  7.9 107.5 %all-gather.5.cloned.1.call-start = ((), (), s32[]{:S(2)}) async-start(), calls=%async_computation.4 | async-start | bytes 2228224 | tf_op jit(solution)/shard_map/all_gather | solution.py:30
  10.3 170.3 %reduce-scatter.3.cloned.1.call-start = ((), (), s32[]{:S(2)}) async-start(), calls=%async_computation.3 | async-start | bytes 4456448 | tf_op jit(solution)/shard_map/reduce_scatter | solution.py:29
  63.0 3.1 copy-start.10
  64.1 2.0 copy-start.1
  76.1 168.0 %reduce-scatter.5.cloned.1.call-start = ((), (), s32[]{:S(2)}) async-start(), calls=%async_computation.5 | async-start | bytes 4456448 | tf_op jit(solution)/shard_map/reduce_scatter | solution.py:31
  127.1 54.5 %copy-start.2 = (bf16[128,512]{1,0:T(8,128)(2,1)S(1)}, bf16[128,512]{1,0:T(8,128)(2,1)}, u32[]{:S(2)}) copy-start(bf16[128,512]{1,0:T(8,128)(2,1)} %broadcast_select_fusion) | copy-start | bytes 393220
  127.1 55.8 %copy-start.6 = (bf16[128,512]{1,0:T(8,128)(2,1)S(1)}, bf16[128,512]{1,0:T(8,128)(2,1)}, u32[]{:S(2)}) copy-start(bf16[128,512]{1,0:T(8,128)(2,1)} %param.10) | copy-start | bytes 393220
  127.1 119.6 %copy-start.7 = (bf16[512,512]{1,0:T(8,128)(2,1)S(1)}, bf16[512,512]{1,0:T(8,128)(2,1)}, u32[]{:S(2)}) copy-start(bf16[512,512]{1,0:T(8,128)(2,1)} %param.14) | copy-start | bytes 1572868
  127.1 386.5 %all-reduce.3.cloned.1.call-start = ((), (), s32[]{:S(2)}) async-start(), calls=%async_computation.6 | async-start | bytes 6291456 | tf_op jit(solution)/shard_map/psum | solution.py:39
  181.5 65.4 %copy-start.4 = (bf16[128,512]{1,0:T(8,128)(2,1)}, bf16[128,512]{1,0:T(8,128)(2,1)S(1)}, u32[]{:S(2)}) copy-start(bf16[128,512]{1,0:T(8,128)(2,1)S(1)} %negate_convert_fusion) | copy-start | bytes 393220
  182.9 64.0 %copy-start.8 = (bf16[512,512]{1,0:T(8,128)(2,1)S(1)}, bf16[512,512]{1,0:T(8,128)(2,1)}, u32[]{:S(2)}) copy-start(bf16[512,512]{1,0:T(8,128)(2,1)} %param.15) | copy-start | bytes 1572868
  245.3 269.8 %copy-start.9 = (bf16[128,512]{1,0:T(8,128)(2,1)}, bf16[128,512]{1,0:T(8,128)(2,1)S(1)}, u32[]{:S(2)}) copy-start(bf16[128,512]{1,0:T(8,128)(2,1)S(1)} %fusion.9) | copy-start | bytes 393220
  513.7 4.1 copy-start.5
  517.7 2.5 copy-start.3
Sparse Core Ops, SparseCore 0:
  10.4 52.4 all-gather.2
  66.0 49.3 all-gather.4
  117.9 62.5 reduce-scatter.2
  183.0 61.1 reduce-scatter.4
  249.7 263.8 all-reduce.2
where the time goes:
time: 527 us
  waiting for transfers between devices  472 us (90%)
  matrix products  29.8 us (6%)
  between operations  13.9 us (3%)
  local copies, waits for them, and re-layouts  5.61 us (1%)
  other arithmetic  5.46 us (1%)
    psum x1, waiting for transfers between devices, on_device(): own_sum, cross_sum = lax.psum((own_term, cross_local), ('prow', 'pcol'))  266 us
    reduce_scatter x1, waiting for transfers between devices, on_device(): lax.psum_scatter(partial_two, 'pcol', scatter_dimension=0, tiled=True)  59.9 us
    reduce_scatter x1, waiting for transfers between devices, on_device(): lax.psum_scatter(partial_one, 'pcol', scatter_dimension=0, tiled=True)  53.2 us
    all_gather x1, waiting for transfers between devices, on_device(): lax.all_gather(panel_one, 'prow', axis=0, tiled=True)  51.9 us
    all_gather x1, waiting for transfers between devices, on_device(): lax.all_gather(masked_two, 'prow', axis=0, tiled=True)  39.2 us
    dot_general x2, matrix products, accumulate(): return jnp.dot(masked, pieces, preferred_element_type=jnp.float32)  21.7 us
  transfers between devices with their start and end apart: 5, of which 5 were waited for; matrix products, arithmetic and copies ran while one was open for 6% of the time, Pallas kernels for 0%

commit v1 on v0

v1 whole, which is shorter than its diff:
```python
import jax
import jax.numpy as jnp
from jax import lax
from jax.experimental import pallas as pl
from jax.experimental.pallas import tpu as pltpu
from jax.sharding import PartitionSpec as P

MESH = pl.DeviceIdType.MESH
BF = jnp.bfloat16
F32 = jnp.float32
CHUNKS = 4
HALF = 128
WIDE = 256
BLK = 128
W = 512


def dot(a, b):
    return jnp.dot(a, b, preferred_element_type=F32)


def dot_t(a, b):
    return lax.dot_general(a, b, (((0,), (0,)), ((), ())), preferred_element_type=F32)


def kernel(
    m_hbm, pat, p1, p2, ptop, struct, d1, d2,
    o_inv1, o_c1, o_top, o_inv2, o_c2,
    raw, tall, ms, g, keep, csnd, crcv, rsnd, rrcv, p2m, red, quad,
    ta, sa1, ra1, sa2, ra2, ra3, ga, gca,
    tb, sb1, rb1, sb2, rb2, rb3, gb, gcb,
    m_sem, ag1_sem, ag2_sem, agf_sem, ags_sem, c_sem, cs_sem, r_sem, rs_sem, ar_sem, ars_sem,
):
    me_r = lax.axis_index("prow")
    me_c = lax.axis_index("pcol")
    x, y, z, k = me_r // 4, me_r % 4, me_c // 2, me_c % 2
    other = 1 - k

    def at(dx, dy, dz, dk):
        return (
            ((x + dx) % 4) * 4 + (y + dy) % 4,
            ((z + dz) % 8) * 2 + (k + dk) % 2,
        )

    plane = [(dx, dy, 0, 0) for dx in range(4) for dy in range(4) if dx or dy]
    column = [(0, 0, dz, 0) for dz in range(1, 8)]
    mate = [(0, 0, 0, 1)]

    def send(src, dst, ssem, rsem, off):
        pltpu.make_async_remote_copy(
            src_ref=src, dst_ref=dst, send_sem=ssem, recv_sem=rsem,
            device_id=at(*off), device_id_type=MESH,
        ).start()

    def wait(ref, sem):
        pltpu.make_async_copy(ref, ref, sem).wait()

    def row_block(i):
        return 2 * i + other if i < 8 else 2 * (i - 8) + k

    for i in range(16):
        pltpu.make_async_copy(m_hbm.at[row_block(i)], raw.at[i], m_sem.at[i]).start()

    barrier = pltpu.get_barrier_semaphore()
    peers = plane + column + mate
    for off in peers:
        pl.semaphore_signal(barrier, inc=1, device_id=at(*off), device_id_type=MESH)

    flags = jnp.broadcast_to(struct[...], (BLK, BLK)) > 0
    eye = lax.broadcasted_iota(jnp.int32, (BLK, BLK), 0) == lax.broadcasted_iota(
        jnp.int32, (BLK, BLK), 1
    )
    pick = jnp.where(flags & eye, 1.0, 0.0).astype(BF)
    p2m[...] = dot(pick, p2[...]).astype(BF)
    for s in range(CHUNKS):
        for h in range(2):
            src = p1 if s < 2 else p2m
            c0 = (s % 2) * WIDE + h * HALF
            g[s, h, x, y] = src[:, c0 : c0 + HALF]

    pl.semaphore_wait(barrier, len(peers))

    def step_along(h, first):
        along_x = (h == 0) == first
        return (lambda d: (d, 0, 0, 0)) if along_x else (lambda d: (0, d, 0, 0))

    def gather1(s):
        for h in range(2):
            off = step_along(h, True)
            blk = g.at[s, h, x, y]
            for d in (1, 3, 2):
                send(blk, blk, ags_sem.at[s, h], ag1_sem.at[s, h], off(d))

    def line(s, h, d, lo, n):
        if h == 0:
            return g.at[s, h, pl.ds(lo, n), (y + d) % 4]
        return g.at[s, h, (x + d) % 4, pl.ds(lo, n)]

    def gather2(s):
        for h in range(2):
            wait(line(s, h, 0, 0, 3), ag1_sem.at[s, h])
            off = step_along(h, False)
            mine = line(s, h, 0, 0, 4)
            send(mine, mine, ags_sem.at[s, h], ag2_sem.at[s, h, 0], off(1))
            send(mine, mine, ags_sem.at[s, h], ag2_sem.at[s, h, 1], off(3))

    def gather3(s):
        for h in range(2):
            off = step_along(h, False)
            wait(line(s, h, 3, 0, 4), ag2_sem.at[s, h, 0])
            low = line(s, h, 3, 0, 2)
            send(low, low, ags_sem.at[s, h], agf_sem.at[s, h], off(1))
            wait(line(s, h, 1, 0, 4), ag2_sem.at[s, h, 1])
            high = line(s, h, 1, 2, 2)
            send(high, high, ags_sem.at[s, h], agf_sem.at[s, h], off(3))

    def gathered(s):
        for h in range(2):
            wait(line(s, h, 2, 0, 4), agf_sem.at[s, h])

    def relayout(lo, hi):
        @pl.loop(lo, hi)
        def _(i):
            rb = jnp.where(i < 8, 2 * i + other, 2 * (i - 8) + k)
            pltpu.make_async_copy(m_hbm.at[rb], raw.at[i], m_sem.at[i]).wait()
            tall[...] = raw[i].astype(F32)
            for a in range(16):
                v = tall[pl.ds(a, BLK, stride=16), :]
                v = jnp.where(pat[rb, a] > 0, v, 0.0)
                ms[pl.ds(i * BLK, BLK), a * BLK : (a + 1) * BLK] = v.astype(BF)

    def panel(s):
        return jnp.concatenate([g[s, h].reshape(2048, HALF) for h in range(2)], axis=1)

    def product(s, tile):
        acc = dot(ms[tile * 1024 : (tile + 1) * 1024, :], panel(s)).reshape(8, BLK, WIDE)
        if tile == 0:
            csnd[s] = acc.astype(BF)
            send(csnd.at[s], crcv.at[s], cs_sem.at[s], c_sem.at[s], mate[0])
        else:
            keep[s] = acc

    def cores(s):
        wait(crcv.at[s], c_sem.at[s])

    def own(s, b, h):
        c = slice(h * HALF, (h + 1) * HALF)
        return keep[s, b, :, c] + crcv[s, b, :, c].astype(F32)

    def slots(t):
        return (0, 1) if t == 1 else (2 * t - 3, 2)

    def ring(s, t):
        for way in range(2):
            if t > 1:
                lo, n = slots(t - 1)
                wait(rrcv.at[s, way, pl.ds(lo, n)], r_sem.at[s, way, t - 2])
        if t == 5:
            for h in range(2):
                red[s, h] = own(s, z, h) + rrcv[s, 0, 5 + h].astype(F32) + rrcv[s, 1, 5 + h].astype(F32)
            return
        for way in range(2):
            d = 5 - t if way == 0 else 8 - (5 - t)
            b = (z + d) % 8
            lo, n = slots(t)
            for h in range(2):
                if t == 1:
                    if h == way:
                        rsnd[s, way, 0] = own(s, b, h).astype(BF)
                    continue
                v = own(s, b, h)
                if t > 2:
                    v = v + rrcv[s, way, slots(t - 1)[0] + h].astype(F32)
                elif h == way:
                    v = v + rrcv[s, way, 0].astype(F32)
                rsnd[s, way, lo + h] = v.astype(BF)
            send(
                rsnd.at[s, way, pl.ds(lo, n)], rrcv.at[s, way, pl.ds(lo, n)],
                rs_sem.at[s], r_sem.at[s, way, t - 1], (0, 0, 1 if way == 0 else 7, 0),
            )

    def sum1(q, t32, s1, r1):
        s1[...] = t32[:, pl.ds(pl.multiple_of(other * 256, 256), 256), :].astype(BF)
        send(s1, r1, ars_sem.at[q, 0], ar_sem.at[q, 0], mate[0])

    def sum2(q, t32, r1, s2, r2):
        wait(r1, ar_sem.at[q, 0])
        n = t32.shape[0]
        for m in range(n):
            v = t32[m, pl.ds(pl.multiple_of(k * 256, 256), 256), :] + r1[m].astype(F32)
            s2[:, m] = v.astype(BF).reshape(16, 16, W)
        for off in plane:
            j = ((x + off[0]) % 4) * 4 + (y + off[1]) % 4
            send(s2.at[j], r2.at[me_r], ars_sem.at[q, 1], ar_sem.at[q, 1], off)
        r2[me_r] = s2[me_r]

    def sum3(q, r2, r3):
        wait(r2.at[pl.ds(0, 15)], ar_sem.at[q, 1])
        v = r2[0].astype(F32)
        for j in range(1, 16):
            v = v + r2[j].astype(F32)
        r3[z] = v.astype(BF)
        for off in column:
            send(r3.at[z], r3.at[z], ars_sem.at[q, 2], ar_sem.at[q, 2], off)

    def sum4(q, r3):
        wait(r3.at[pl.ds(0, 7)], ar_sem.at[q, 2])
        v = r3[0].astype(F32)
        for j in range(1, 8):
            v = v + r3[j].astype(F32)
        return v

    def spread(q, ga_):
        for off in plane:
            send(ga_.at[me_r], ga_.at[me_r], ars_sem.at[q, 3], ar_sem.at[q, 3], off)

    def swap(q, ga_, gc_):
        wait(ga_.at[pl.ds(0, 15)], ar_sem.at[q, 3])
        send(ga_, gc_, ars_sem.at[q, 4], ar_sem.at[q, 4], mate[0])

    def lay(out, ga_, gc_, m):
        out[pl.ds(pl.multiple_of(k * 256, 256), 256), :] = ga_[:, m].reshape(256, W)
        out[pl.ds(pl.multiple_of(other * 256, 256), 256), :] = gc_[:, m].reshape(256, W)

    my_rows = pl.ds(pl.multiple_of(k * 256 + me_r * 16, 16), 16)

    def first_rows():
        r = jnp.concatenate(
            [jnp.concatenate([red[s, h] for h in range(2)], axis=1) for s in range(2)], axis=1
        )
        o_inv1[...] = (-r).astype(BF)
        ta[0] = dot_t(p1[...], o_inv1[...])
        ta[1] = dot_t(o_inv1[...], p2m[...])
        sum1(0, ta, sa1, ra1)

    def second_rows():
        r = jnp.concatenate(
            [jnp.concatenate([red[s, h] for h in range(2)], axis=1) for s in range(2, 4)], axis=1
        )
        low = -(r + dot(o_inv1[...], ptop[...]))
        kept = dot(pick, jnp.ones((BLK, W), BF)) > 0.5
        o_inv2[...] = jnp.where(kept, low, 0.0).astype(BF)
        tb[0] = dot_t(p2m[...], o_inv2[...])
        sum1(1, tb, sb1, rb1)

    def first_corner():
        v = sum4(0, ra3)
        s1 = d1[my_rows, :].astype(F32) - v[0]
        hi = s1.astype(BF)
        rest = s1 - hi.astype(F32)
        mid = rest.astype(BF)
        low = (rest - mid.astype(F32)).astype(BF)
        t = ptop[...]
        top = dot(hi, t) + (dot(mid, t) + dot(low, t))
        ga[me_r, 0] = hi
        ga[me_r, 1] = (-(top + v[1])).astype(BF)
        spread(0, ga)

    def first_done():
        wait(gca, ar_sem.at[0, 4])
        lay(o_c1, ga, gca, 0)
        lay(o_top, ga, gca, 1)
        quad[...] = dot_t(ptop[...], o_top[...])

    def second_corner():
        v = sum4(1, rb3)
        gb[me_r, 0] = (d2[my_rows, :].astype(F32) - quad[my_rows, :] - v[0]).astype(BF)
        spread(1, gb)

    gather1(0)
    gather1(1)
    relayout(0, 4)
    gather2(0)
    gather1(2)
    relayout(4, 9)
    gather2(1)
    relayout(9, 16)
    gather3(0)
    gather2(2)
    gather1(3)
    gathered(0)
    product(0, 0)
    gather3(1)
    product(0, 1)
    gather2(3)
    cores(0)
    ring(0, 1)
    gathered(1)
    product(1, 0)
    ring(0, 2)
    gather3(2)
    product(1, 1)
    ring(0, 3)
    cores(1)
    ring(1, 1)
    gathered(2)
    product(2, 0)
    ring(0, 4)
    ring(1, 2)
    gather3(3)
    product(2, 1)
    ring(0, 5)
    ring(1, 3)
    cores(2)
    ring(2, 1)
    gathered(3)
    product(3, 0)
    ring(1, 4)
    ring(2, 2)
    product(3, 1)
    cores(3)
    ring(3, 1)
    ring(1, 5)
    first_rows()
    ring(2, 3)
    ring(3, 2)
    sum2(0, ta, ra1, sa2, ra2)
    ring(2, 4)
    ring(3, 3)
    sum3(0, ra2, ra3)
    ring(2, 5)
    ring(3, 4)
    first_corner()
    ring(3, 5)
    second_rows()
    swap(0, ga, gca)
    sum2(1, tb, rb1, sb2, rb2)
    first_done()
    sum3(1, rb2, rb3)
    second_corner()
    swap(1, gb, gcb)

    for s in range(CHUNKS):
        for h in range(2):
            wait(raw.at[0, pl.ds(0, 15 * BLK)], ags_sem.at[s, h])
        wait(csnd.at[s], cs_sem.at[s])
        wait(rsnd.at[s], rs_sem.at[s])
    for q, s1, s2, r3, g_ in ((0, sa1, sa2, ra3, ga), (1, sb1, sb2, rb3, gb)):
        wait(s1, ars_sem.at[q, 0])
        wait(s2.at[pl.ds(0, 15)], ars_sem.at[q, 1])
        wait(r3.at[pl.ds(0, 7)], ars_sem.at[q, 2])
        wait(g_.at[pl.ds(0, 15)], ars_sem.at[q, 3])
        wait(g_, ars_sem.at[q, 4])
    wait(gcb, ar_sem.at[1, 4])
    lay(o_c2, gb, gcb, 0)


def on_device(known_inverse, pattern, panel_one, panel_two, panel_top, structure, diag_one, diag_two):
    vm, sm, hbm = (pl.BlockSpec(memory_space=s) for s in (pltpu.VMEM, pltpu.SMEM, pl.ANY))
    V, S = pltpu.VMEM, pltpu.SemaphoreType.DMA

    def sums(n, no):
        return [
            V((n, W, W), F32),
            V((n, 256, W), BF), V((n, 256, W), BF),
            V((16, n, 16, W), BF), V((16, n, 16, W), BF),
            V((8, n, 16, W), BF),
            V((16, no, 16, W), BF), V((16, no, 16, W), BF),
        ]

    corner = jax.ShapeDtypeStruct((W, W), BF)
    rows = jax.ShapeDtypeStruct((BLK, W), BF)
    return pl.pallas_call(
        kernel,
        out_shape=(rows, corner, corner, rows, corner),
        in_specs=[hbm, sm, vm, vm, vm, vm, vm, vm],
        out_specs=(vm,) * 5,
        scratch_shapes=[
            V((16, 2048, BLK), BF), V((2048, BLK), F32), V((2048, 2048), BF),
            V((CHUNKS, 2, 4, 4, BLK, HALF), BF),
            V((CHUNKS, 8, BLK, WIDE), F32), V((CHUNKS, 8, BLK, WIDE), BF), V((CHUNKS, 8, BLK, WIDE), BF),
            V((CHUNKS, 2, 7, BLK, HALF), BF), V((CHUNKS, 2, 7, BLK, HALF), BF),
            V((BLK, W), BF), V((CHUNKS, 2, BLK, HALF), F32), V((W, W), F32),
            *sums(2, 2), *sums(1, 1),
            S((16,)), S((CHUNKS, 2)), S((CHUNKS, 2, 2)), S((CHUNKS, 2)), S((CHUNKS, 2)),
            S((CHUNKS,)), S((CHUNKS,)), S((CHUNKS, 2, 4)), S((CHUNKS,)), S((2, 5)), S((2, 5)),
        ],
        compiler_params=pltpu.CompilerParams(
            collective_id=0, has_side_effects=True, vmem_limit_bytes=60 * 2**20
        ),
        cost_estimate=pl.CostEstimate(flops=2 * 2048 * 2048 * 1024, bytes_accessed=12 * 2**20, transcendentals=0),
        name="inverse",
    )(
        known_inverse.reshape(16, 2048, BLK),
        pattern.reshape(16, 16),
        panel_one, panel_two, panel_top, structure.reshape(1, BLK), diag_one, diag_two,
    )


def solution(mesh):
    in_specs = (
        P("prow", None, "pcol", None), P("prow", None, "pcol", None),
        P(("prow", "pcol"), None), P(("prow", "pcol"), None),
        P(), P(("prow", "pcol")), P(), P(),
    )
    out_specs = (P(("prow", "pcol"), None), P(), P(), P(("prow", "pcol"), None), P())
    return jax.shard_map(on_device, mesh=mesh, in_specs=in_specs, out_specs=out_specs, check_vma=False)
```

time: 527 us -> 120 us (0.23)
  waiting for transfers between devices: 472 us -> 0 us
  Pallas kernels: 0 us -> 108 us
  matrix products: 29.8 us -> 0 us
  between operations: 13.9 us -> 0.64 us
  other arithmetic: 5.46 us -> 0 us
    psum x1 -> x0, waiting for transfers between devices: 266 us -> none  [on_device(): own_sum, cross_sum = lax.psum((own_term, cross_local), ('prow', 'pcol'))]
    reduce_scatter x2 -> x0, waiting for transfers between devices: 113 us -> none  [the longest x1 59.9 us: on_device(): lax.psum_scatter(partial_two, 'pcol', scatter_dimension=0, tiled=True)]
    pallas_call x0 -> x1, Pallas kernels: none -> 108 us  [on_device(): pl.pallas_call(kernel, out_shape=(rows, corner, corner, rows, corner), in...]
    all_gather x2 -> x0, waiting for transfers between devices: 91.1 us -> none  [the longest x1 51.9 us: on_device(): lax.all_gather(panel_one, 'prow', axis=0, tiled=True)]
    dot_general x8 -> x0, matrix products: 29.8 us -> none  [the longest x2 21.7 us: accumulate(): return jnp.dot(masked, pieces, preferred_element_type=jnp.float32)]
  transfers between devices with their start and end apart: 5 -> 0, of which waited for: 5 -> 0; matrix products, arithmetic and copies ran while one was open for 6% -> 0% of each run, Pallas kernels for 0% -> 0%
where the time goes in v1:
time: 120 us; the launch traced here: 117 us
  Pallas kernels  108 us (90%)
  local copies, waits for them, and re-layouts  8.74 us (7%)
    pallas_call x1, Pallas kernels, on_device(): pl.pallas_call(kernel, out_shape=(rows, corner, corner, rows, corner), in...  108 us
    unnamed x5, local copies, waits for them, and re-layouts  8.74 us

profile of v1, /device:TPU:8, one launch (start us, length us, event | category | flops | bytes accessed | tf_op | source)
XLA Modules:
  0.0 117.4 jit_solution(8716021061300120448)
XLA Ops:
  0.6 108.0 %inverse.1 = (bf16[128,512]{1,0:T(8,128)(2,1)}, bf16[512,512]{1,0:T(8,128)(2,1)}, bf16[512,512]{1,0:T(8,128)(2,1)}, bf16[128,512]{1,0:T(8,128)(2,1)}, bf16[512,512]{1,0:T(8,128)(2,1)}) custom-call(bf16[16,2048,128]{2,1,0:T(8,128)(2,1)} %bitcast.3, s32[16,16]{1,0:T(8,128)} %bitcast.4, bf16[128,512]{1,0:T(8,128)(2,1)} %p1.1, bf16[128,512]{1,0:T(8,128)(2,1)} %p2.1, ...), custom_call_target="tpu_custom_call" | custom-call | flops 8589934592 | bytes 12582912 | tf_op jit(solution)/shard_map/inverse/pallas_call | solution.py:363
  108.6 1.6 %copy.18 = bf16[128,512]{1,0:T(8,128)(2,1)} copy(bf16[128,512]{1,0:T(8,128)(2,1)} %get-tuple-element.10) | data formatting | bytes 262144
  110.2 1.9 %copy.19 = bf16[512,512]{1,0:T(8,128)(2,1)} copy(bf16[512,512]{1,0:T(8,128)(2,1)} %get-tuple-element.11) | data formatting | bytes 1048576
  112.1 1.9 %copy.20 = bf16[512,512]{1,0:T(8,128)(2,1)} copy(bf16[512,512]{1,0:T(8,128)(2,1)} %get-tuple-element.12) | data formatting | bytes 1048576
  113.9 1.6 %copy.21 = bf16[128,512]{1,0:T(8,128)(2,1)} copy(bf16[128,512]{1,0:T(8,128)(2,1)} %get-tuple-element.13) | data formatting | bytes 262144
  115.5 1.9 %copy.22 = bf16[512,512]{1,0:T(8,128)(2,1)} copy(bf16[512,512]{1,0:T(8,128)(2,1)} %get-tuple-element.14) | data formatting | bytes 1048576

commit v2 on v1

--- a/solution.py
+++ b/solution.py
@@ -26,10 +26,10 @@
 def kernel(
     m_hbm, pat, p1, p2, ptop, struct, d1, d2,
     o_inv1, o_c1, o_top, o_inv2, o_c2,
-    raw, tall, ms, g, keep, csnd, crcv, rsnd, rrcv, p2m, red, quad,
+    raw, tall, ms, g, zg, keep, csnd, crcv, rsnd, rrcv, red, base,
     ta, sa1, ra1, sa2, ra2, ra3, ga, gca,
-    tb, sb1, rb1, sb2, rb2, rb3, gb, gcb,
-    m_sem, ag1_sem, ag2_sem, agf_sem, ags_sem, c_sem, cs_sem, r_sem, rs_sem, ar_sem, ars_sem,
+    tb, sb, rb, sc, rc, gb, gcb,
+    m_sem, ag1_sem, ag2_sem, agf_sem, ags_sem, zg_sem, zs_sem, c_sem, cs_sem, r_sem, rs_sem, ar_sem, ars_sem, br_sem, bs_sem,
 ):
     me_r = lax.axis_index("prow")
     me_c = lax.axis_index("pcol")
@@ -45,6 +45,7 @@
     plane = [(dx, dy, 0, 0) for dx in range(4) for dy in range(4) if dx or dy]
     column = [(0, 0, dz, 0) for dz in range(1, 8)]
     mate = [(0, 0, 0, 1)]
+    tower = [(0, 0, dz, dk) for dk in (0, 1) for dz in range(8) if dz or dk]
 
     def send(src, dst, ssem, rsem, off):
         pltpu.make_async_remote_copy(
@@ -62,7 +63,7 @@
         pltpu.make_async_copy(m_hbm.at[row_block(i)], raw.at[i], m_sem.at[i]).start()
 
     barrier = pltpu.get_barrier_semaphore()
-    peers = plane + column + mate
+    peers = plane + tower
     for off in peers:
         pl.semaphore_signal(barrier, inc=1, device_id=at(*off), device_id_type=MESH)
 
@@ -71,12 +72,12 @@
         jnp.int32, (BLK, BLK), 1
     )
     pick = jnp.where(flags & eye, 1.0, 0.0).astype(BF)
-    p2m[...] = dot(pick, p2[...]).astype(BF)
-    for s in range(CHUNKS):
+    zg[0, z] = p1[...]
+    zg[1, z] = dot(pick, p2[...]).astype(BF)
+    for s in range(2):
         for h in range(2):
-            src = p1 if s < 2 else p2m
-            c0 = (s % 2) * WIDE + h * HALF
-            g[s, h, x, y] = src[:, c0 : c0 + HALF]
+            c0 = s * WIDE + h * HALF
+            g[s, h, x, y] = p1[:, c0 : c0 + HALF]
 
     pl.semaphore_wait(barrier, len(peers))
 
@@ -117,6 +118,26 @@
     def gathered(s):
         for h in range(2):
             wait(line(s, h, 2, 0, 4), agf_sem.at[s, h])
+
+    def second_panel():
+        v = zg[1, z].astype(F32) - dot(p1[...], ptop[...])
+        for s in range(2, CHUNKS):
+            for h in range(2):
+                c0 = (s - 2) * WIDE + h * HALF
+                g[s, h, x, y] = v[:, c0 : c0 + HALF].astype(BF)
+
+    def rows_along(t, p):
+        for way in range(2):
+            d = t - 1 if way else -(t - 1)
+            blk = zg.at[p, (z + d + 8) % 8]
+            half = blk.at[pl.ds(64 * way, 64)]
+            if t > 1:
+                got = half if t == 5 else blk
+                wait(got, zg_sem.at[p, way, t - 2])
+            if t == 5:
+                continue
+            src = half if t == 4 else blk
+            send(src, src, zs_sem.at[p], zg_sem.at[p, way, t - 1], (0, 0, 7 if way else 1, 0))
 
     def relayout(lo, hi):
         @pl.loop(lo, hi)
@@ -142,10 +163,21 @@
 
     def cores(s):
         wait(crcv.at[s], c_sem.at[s])
+        keep[s] = keep[s] + crcv[s].astype(F32)
+
+    def part(s):
+        v = keep[s].astype(BF).reshape(1024, WIDE)
+        c = slice((s % 2) * WIDE, (s % 2 + 1) * WIDE)
+        two = zg[1].reshape(1024, W)
+        if s < 2:
+            ta[0, :, c] = dot_t(zg[0].reshape(1024, W), v)
+            ta[1, c, :] = dot_t(v, two)
+        else:
+            tb[s - 2] = tb[s - 2] + dot_t(two, v)
 
     def own(s, b, h):
         c = slice(h * HALF, (h + 1) * HALF)
-        return keep[s, b, :, c] + crcv[s, b, :, c].astype(F32)
+        return keep[s, b, :, c]
 
     def slots(t):
         return (0, 1) if t == 1 else (2 * t - 3, 2)
@@ -229,23 +261,17 @@
             [jnp.concatenate([red[s, h] for h in range(2)], axis=1) for s in range(2)], axis=1
         )
         o_inv1[...] = (-r).astype(BF)
-        ta[0] = dot_t(p1[...], o_inv1[...])
-        ta[1] = dot_t(o_inv1[...], p2m[...])
-        sum1(0, ta, sa1, ra1)
 
     def second_rows():
         r = jnp.concatenate(
             [jnp.concatenate([red[s, h] for h in range(2)], axis=1) for s in range(2, 4)], axis=1
         )
-        low = -(r + dot(o_inv1[...], ptop[...]))
         kept = dot(pick, jnp.ones((BLK, W), BF)) > 0.5
-        o_inv2[...] = jnp.where(kept, low, 0.0).astype(BF)
-        tb[0] = dot_t(p2m[...], o_inv2[...])
-        sum1(1, tb, sb1, rb1)
+        o_inv2[...] = jnp.where(kept, -r, 0.0).astype(BF)
 
     def first_corner():
         v = sum4(0, ra3)
-        s1 = d1[my_rows, :].astype(F32) - v[0]
+        s1 = d1[my_rows, :].astype(F32) + v[0]
         hi = s1.astype(BF)
         rest = s1 - hi.astype(F32)
         mid = rest.astype(BF)
@@ -253,96 +279,174 @@
         t = ptop[...]
         top = dot(hi, t) + (dot(mid, t) + dot(low, t))
         ga[me_r, 0] = hi
-        ga[me_r, 1] = (-(top + v[1])).astype(BF)
+        ga[me_r, 1] = (v[1] - top).astype(BF)
         spread(0, ga)
 
     def first_done():
         wait(gca, ar_sem.at[0, 4])
         lay(o_c1, ga, gca, 0)
         lay(o_top, ga, gca, 1)
-        quad[...] = dot_t(ptop[...], o_top[...])
-
-    def second_corner():
-        v = sum4(1, rb3)
-        gb[me_r, 0] = (d2[my_rows, :].astype(F32) - quad[my_rows, :] - v[0]).astype(BF)
-        spread(1, gb)
+
+    def fixed_part():
+        t = ptop[...]
+        base[...] = d2[...].astype(F32) + dot_t(t, dot(d1[...], t).astype(BF))
+
+    def first_part():
+        t = ptop[...]
+        u = dot_t(t, (dot(ta[0].astype(BF), t) - ta[1]).astype(BF))
+        tb[0] = u[:, :WIDE]
+        tb[1] = u[:, WIDE:]
+
+    def low1(c):
+        for half in range(2):
+            sb[c, :, half] = tb[c, half * 256 : (half + 1) * 256].astype(BF).reshape(16, 16, WIDE)
+        for off in plane:
+            j = ((x + off[0]) % 4) * 4 + (y + off[1]) % 4
+            send(sb.at[c, j], rb.at[c, me_r], bs_sem.at[c, 0], br_sem.at[c, 0], off)
+        rb[c, me_r] = sb[c, me_r]
+
+    def low2(c):
+        wait(rb.at[c, pl.ds(0, 15)], br_sem.at[c, 0])
+        v = rb[c, 0].astype(F32)
+        for j in range(1, 16):
+            v = v + rb[c, j].astype(F32)
+        sc[c] = v.astype(BF)
+        for off in tower:
+            to = k if off[3] == 0 else other
+            send(sc.at[c, to], rc.at[c, me_c], bs_sem.at[c, 1], br_sem.at[c, 1], off)
+        rc[c, me_c] = sc[c, k]
+
+    def low3(c):
+        wait(rc.at[c, pl.ds(0, 15)], br_sem.at[c, 1])
+        v = base[my_rows, c * WIDE : (c + 1) * WIDE]
+        for j in range(16):
+            v = v + rc[c, j].astype(F32)
+        gb[c, me_r] = v.astype(BF)
+        for off in plane:
+            send(gb.at[c, me_r], gb.at[c, me_r], bs_sem.at[c, 2], br_sem.at[c, 2], off)
+
+    def low4(c):
+        wait(gb.at[c, pl.ds(0, 15)], br_sem.at[c, 2])
+        send(gb.at[c], gcb.at[c], bs_sem.at[c, 3], br_sem.at[c, 3], mate[0])
+
+    def low5(c):
+        wait(gcb.at[c], br_sem.at[c, 3])
+        cols = slice(c * WIDE, (c + 1) * WIDE)
+        o_c2[pl.ds(pl.multiple_of(k * 256, 256), 256), cols] = gb[c].reshape(256, WIDE)
+        o_c2[pl.ds(pl.multiple_of(other * 256, 256), 256), cols] = gcb[c].reshape(256, WIDE)
 
     gather1(0)
+    rows_along(1, 0)
     gather1(1)
-    relayout(0, 4)
+    rows_along(1, 1)
+    second_panel()
+    relayout(0, 3)
     gather2(0)
+    rows_along(2, 0)
+    relayout(3, 5)
+    gather2(1)
     gather1(2)
-    relayout(4, 9)
-    gather2(1)
-    relayout(9, 16)
+    relayout(5, 9)
+    rows_along(2, 1)
+    relayout(9, 12)
+    rows_along(3, 0)
     gather3(0)
     gather2(2)
     gather1(3)
+    relayout(12, 16)
+    rows_along(3, 1)
+    gather3(1)
+    gather2(3)
     gathered(0)
     product(0, 0)
-    gather3(1)
+    rows_along(4, 0)
+    gather3(2)
     product(0, 1)
-    gather2(3)
+    rows_along(4, 1)
+    gathered(1)
+    product(1, 0)
+    gather3(3)
     cores(0)
     ring(0, 1)
-    gathered(1)
-    product(1, 0)
-    ring(0, 2)
-    gather3(2)
     product(1, 1)
-    ring(0, 3)
+    rows_along(5, 0)
+    rows_along(5, 1)
+    part(0)
     cores(1)
+    part(1)
+    sum1(0, ta, sa1, ra1)
     ring(1, 1)
     gathered(2)
     product(2, 0)
-    ring(0, 4)
+    ring(0, 2)
+    sum2(0, ta, ra1, sa2, ra2)
     ring(1, 2)
-    gather3(3)
     product(2, 1)
-    ring(0, 5)
-    ring(1, 3)
+    ring(0, 3)
+    first_part()
     cores(2)
+    part(2)
+    low1(0)
     ring(2, 1)
     gathered(3)
     product(3, 0)
+    ring(0, 4)
+    ring(1, 3)
+    product(3, 1)
+    sum3(0, ra2, ra3)
+    cores(3)
+    part(3)
+    low1(1)
+    ring(3, 1)
+    ring(2, 2)
+    low2(0)
+    fixed_part()
+    ring(0, 5)
     ring(1, 4)
-    ring(2, 2)
-    product(3, 1)
-    cores(3)
-    ring(3, 1)
+    low2(1)
+    first_corner()
+    ring(2, 3)
+    ring(3, 2)
     ring(1, 5)
     first_rows()
-    ring(2, 3)
-    ring(3, 2)
-    sum2(0, ta, ra1, sa2, ra2)
+    low3(0)
     ring(2, 4)
     ring(3, 3)
-    sum3(0, ra2, ra3)
+    low3(1)
+    swap(0, ga, gca)
     ring(2, 5)
     ring(3, 4)
-    first_corner()
+    low4(0)
+    low4(1)
+    first_done()
+    low5(0)
     ring(3, 5)
     second_rows()
-    swap(0, ga, gca)
-    sum2(1, tb, rb1, sb2, rb2)
-    first_done()
-    sum3(1, rb2, rb3)
-    second_corner()
-    swap(1, gb, gcb)
 
     for s in range(CHUNKS):
         for h in range(2):
             wait(raw.at[0, pl.ds(0, 15 * BLK)], ags_sem.at[s, h])
         wait(csnd.at[s], cs_sem.at[s])
         wait(rsnd.at[s], rs_sem.at[s])
-    for q, s1, s2, r3, g_ in ((0, sa1, sa2, ra3, ga), (1, sb1, sb2, rb3, gb)):
+    for p in range(2):
+        wait(zg.at[p, pl.ds(0, 7)], zs_sem.at[p])
+    for q, s1, s2, r3, g_ in ((0, sa1, sa2, ra3, ga),):
         wait(s1, ars_sem.at[q, 0])
         wait(s2.at[pl.ds(0, 15)], ars_sem.at[q, 1])
         wait(r3.at[pl.ds(0, 7)], ars_sem.at[q, 2])
         wait(g_.at[pl.ds(0, 15)], ars_sem.at[q, 3])
         wait(g_, ars_sem.at[q, 4])
-    wait(gcb, ar_sem.at[1, 4])
-    lay(o_c2, gb, gcb, 0)
+    for c in range(2):
+        wait(sb.at[c, pl.ds(0, 15)], bs_sem.at[c, 0])
+        wait(rc.at[c, pl.ds(0, 15)], bs_sem.at[c, 1])
+        wait(gb.at[c, pl.ds(0, 15)], bs_sem.at[c, 2])
+        wait(gb.at[c], bs_sem.at[c, 3])
+    low5(1)
+
+
+def hand_out(*refs):
+    for i in range(5):
+        refs[5 + i][...] = refs[i][...]
 
 
 def on_device(known_inverse, pattern, panel_one, panel_two, panel_top, structure, diag_one, diag_two):
@@ -360,20 +464,24 @@
 
     corner = jax.ShapeDtypeStruct((W, W), BF)
     rows = jax.ShapeDtypeStruct((BLK, W), BF)
-    return pl.pallas_call(
+    parts = pl.pallas_call(
         kernel,
         out_shape=(rows, corner, corner, rows, corner),
         in_specs=[hbm, sm, vm, vm, vm, vm, vm, vm],
         out_specs=(vm,) * 5,
         scratch_shapes=[
             V((16, 2048, BLK), BF), V((2048, BLK), F32), V((2048, 2048), BF),
-            V((CHUNKS, 2, 4, 4, BLK, HALF), BF),
+            V((CHUNKS, 2, 4, 4, BLK, HALF), BF), V((2, 8, BLK, W), BF),
             V((CHUNKS, 8, BLK, WIDE), F32), V((CHUNKS, 8, BLK, WIDE), BF), V((CHUNKS, 8, BLK, WIDE), BF),
             V((CHUNKS, 2, 7, BLK, HALF), BF), V((CHUNKS, 2, 7, BLK, HALF), BF),
-            V((BLK, W), BF), V((CHUNKS, 2, BLK, HALF), F32), V((W, W), F32),
-            *sums(2, 2), *sums(1, 1),
+            V((CHUNKS, 2, BLK, HALF), F32), V((W, W), F32),
+            *sums(2, 2),
+            V((2, W, WIDE), F32), V((2, 16, 2, 16, WIDE), BF), V((2, 16, 2, 16, WIDE), BF),
+            V((2, 2, 16, WIDE), BF), V((2, 16, 16, WIDE), BF), V((2, 16, 16, WIDE), BF), V((2, 16, 16, WIDE), BF),
             S((16,)), S((CHUNKS, 2)), S((CHUNKS, 2, 2)), S((CHUNKS, 2)), S((CHUNKS, 2)),
-            S((CHUNKS,)), S((CHUNKS,)), S((CHUNKS, 2, 4)), S((CHUNKS,)), S((2, 5)), S((2, 5)),
+            S((2, 2, 4)), S((2,)),
+            S((CHUNKS,)), S((CHUNKS,)), S((CHUNKS, 2, 4)), S((CHUNKS,)), S((1, 5)), S((1, 5)),
+            S((2, 4)), S((2, 4)),
         ],
         compiler_params=pltpu.CompilerParams(
             collective_id=0, has_side_effects=True, vmem_limit_bytes=60 * 2**20
@@ -385,6 +493,13 @@
         pattern.reshape(16, 16),
         panel_one, panel_two, panel_top, structure.reshape(1, BLK), diag_one, diag_two,
     )
+    return pl.pallas_call(
+        hand_out,
+        out_shape=(rows, corner, corner, rows, corner),
+        in_specs=[vm] * 5,
+        out_specs=(vm,) * 5,
+        name="hand_out",
+    )(*parts)
 
 
 def solution(mesh):

time: 120 us -> 89.9 us (0.75)
  Pallas kernels: 108 us -> 87.8 us
  local copies, waits for them, and re-layouts: 8.74 us -> 0 us
    pallas_call x1, Pallas kernels: 108 us -> 85.1 us  [on_device(): pl.pallas_call(kernel, out_shape=(rows, corner, corner, rows, corner), in...]
    unnamed x5 -> x0, local copies, waits for them, and re-layouts: 8.74 us -> none
    pallas_call x0 -> x1, Pallas kernels: none -> 2.7 us  [on_device(): pl.pallas_call(hand_out, out_shape=(rows, corner, corner, rows, corner),...]
where the time goes in v2:
time: 89.9 us; the launch traced here: 88.4 us
  Pallas kernels  87.8 us (98%)
    pallas_call x1, Pallas kernels, on_device(): pl.pallas_call(kernel, out_shape=(rows, corner, corner, rows, corner), in...  85.1 us
    pallas_call x1, Pallas kernels, on_device(): pl.pallas_call(hand_out, out_shape=(rows, corner, corner, rows, corner),...  2.7 us

profile of v2, /device:TPU:8, one launch (start us, length us, event | category | flops | bytes accessed | tf_op | source)
XLA Modules:
  0.0 88.4 jit_solution(6739382707897976102)
XLA Ops:
  0.6 85.1 %inverse.1 = (bf16[128,512]{1,0:T(8,128)(2,1)}, bf16[512,512]{1,0:T(8,128)(2,1)}, bf16[512,512]{1,0:T(8,128)(2,1)}, bf16[128,512]{1,0:T(8,128)(2,1)}, bf16[512,512]{1,0:T(8,128)(2,1)}) custom-call(bf16[16,2048,128]{2,1,0:T(8,128)(2,1)} %bitcast.3, s32[16,16]{1,0:T(8,128)} %bitcast.4, bf16[128,512]{1,0:T(8,128)(2,1)} %p1.1, bf16[128,512]{1,0:T(8,128)(2,1)} %p2.1, ...), custom_call_target="tpu_custom_call" | custom-call | flops 8589934592 | bytes 12582912 | tf_op jit(solution)/shard_map/inverse/pallas_call | solution.py:467
  85.7 2.7 %hand_out.1 = (bf16[128,512]{1,0:T(8,128)(2,1)}, bf16[512,512]{1,0:T(8,128)(2,1)}, bf16[512,512]{1,0:T(8,128)(2,1)}, bf16[128,512]{1,0:T(8,128)(2,1)}, bf16[512,512]{1,0:T(8,128)(2,1)}) custom-call(bf16[128,512]{1,0:T(8,128)(2,1)} %get-tuple-element.10.refs_0_, bf16[512,512]{1,0:T(8,128)(2,1)} %get-tuple-element.11.refs_1_, ...), custom_call_target="tpu_custom_call" | custom-call | tf_op jit(solution)/shard_map/hand_out/pallas_call | solution.py:496

commit v3 on v2

--- a/solution.py
+++ b/solution.py
@@ -338,31 +338,30 @@
     gather1(0)
     rows_along(1, 0)
     gather1(1)
+    second_panel()
     rows_along(1, 1)
-    second_panel()
-    relayout(0, 3)
+    gather1(2)
+    relayout(0, 4)
     gather2(0)
+    gather1(3)
     rows_along(2, 0)
-    relayout(3, 5)
+    relayout(4, 6)
     gather2(1)
-    gather1(2)
-    relayout(5, 9)
     rows_along(2, 1)
-    relayout(9, 12)
+    relayout(6, 12)
     rows_along(3, 0)
     gather3(0)
     gather2(2)
-    gather1(3)
     relayout(12, 16)
-    rows_along(3, 1)
     gather3(1)
     gather2(3)
+    rows_along(3, 1)
     gathered(0)
     product(0, 0)
+    product(0, 1)
     rows_along(4, 0)
+    rows_along(4, 1)
     gather3(2)
-    product(0, 1)
-    rows_along(4, 1)
     gathered(1)
     product(1, 0)
     gather3(3)
@@ -380,36 +379,36 @@
     product(2, 0)
     ring(0, 2)
     sum2(0, ta, ra1, sa2, ra2)
-    ring(1, 2)
     product(2, 1)
     ring(0, 3)
+    ring(1, 2)
     first_part()
+    gathered(3)
+    product(3, 0)
     cores(2)
     part(2)
     low1(0)
     ring(2, 1)
-    gathered(3)
-    product(3, 0)
     ring(0, 4)
     ring(1, 3)
     product(3, 1)
-    sum3(0, ra2, ra3)
     cores(3)
     part(3)
     low1(1)
     ring(3, 1)
     ring(2, 2)
+    sum3(0, ra2, ra3)
     low2(0)
     fixed_part()
     ring(0, 5)
     ring(1, 4)
     low2(1)
-    first_corner()
     ring(2, 3)
     ring(3, 2)
+    first_corner()
+    low3(0)
     ring(1, 5)
     first_rows()
-    low3(0)
     ring(2, 4)
     ring(3, 3)
     low3(1)

time: 89.9 us -> 86.5 us (0.962); the launches traced: 88.4 us -> 86.4 us
  Pallas kernels: 87.8 us -> 85.8 us
    pallas_call x1, Pallas kernels: 85.1 us -> 83.1 us  [on_device(): pl.pallas_call(kernel, out_shape=(rows, corner, corner, rows, corner), in...]
where the time goes in v3:
time: 86.5 us; the launch traced here: 86.4 us
  Pallas kernels  85.8 us (99%)
    pallas_call x1, Pallas kernels, on_device(): pl.pallas_call(kernel, out_shape=(rows, corner, corner, rows, corner), in...  83.1 us
    pallas_call x1, Pallas kernels, on_device(): pl.pallas_call(hand_out, out_shape=(rows, corner, corner, rows, corner),...  2.7 us

profile of v3, /device:TPU:8, one launch (start us, length us, event | category | flops | bytes accessed | tf_op | source)
XLA Modules:
  0.0 86.4 jit_solution(1606097145550258976)
XLA Ops:
  0.6 83.1 %inverse.1 = (bf16[128,512]{1,0:T(8,128)(2,1)}, bf16[512,512]{1,0:T(8,128)(2,1)}, bf16[512,512]{1,0:T(8,128)(2,1)}, bf16[128,512]{1,0:T(8,128)(2,1)}, bf16[512,512]{1,0:T(8,128)(2,1)}) custom-call(bf16[16,2048,128]{2,1,0:T(8,128)(2,1)} %bitcast.3, s32[16,16]{1,0:T(8,128)} %bitcast.4, bf16[128,512]{1,0:T(8,128)(2,1)} %p1.1, bf16[128,512]{1,0:T(8,128)(2,1)} %p2.1, ...), custom_call_target="tpu_custom_call" | custom-call | flops 8589934592 | bytes 12582912 | tf_op jit(solution)/shard_map/inverse/pallas_call | solution.py:466
  83.7 2.7 %hand_out.1 = (bf16[128,512]{1,0:T(8,128)(2,1)}, bf16[512,512]{1,0:T(8,128)(2,1)}, bf16[512,512]{1,0:T(8,128)(2,1)}, bf16[128,512]{1,0:T(8,128)(2,1)}, bf16[512,512]{1,0:T(8,128)(2,1)}) custom-call(bf16[128,512]{1,0:T(8,128)(2,1)} %get-tuple-element.10.refs_0_, bf16[512,512]{1,0:T(8,128)(2,1)} %get-tuple-element.11.refs_1_, ...), custom_call_target="tpu_custom_call" | custom-call | tf_op jit(solution)/shard_map/hand_out/pallas_call | solution.py:495

commit v4 on v3

--- a/solution.py
+++ b/solution.py
@@ -63,7 +63,7 @@
         pltpu.make_async_copy(m_hbm.at[row_block(i)], raw.at[i], m_sem.at[i]).start()
 
     barrier = pltpu.get_barrier_semaphore()
-    peers = plane + tower
+    peers = [o for o in plane if 0 in o[:2]] + [(0, 0, 1, 0), (0, 0, 7, 0)] + mate
     for off in peers:
         pl.semaphore_signal(barrier, inc=1, device_id=at(*off), device_id_type=MESH)
 
@@ -398,11 +398,11 @@
     ring(3, 1)
     ring(2, 2)
     sum3(0, ra2, ra3)
-    low2(0)
-    fixed_part()
     ring(0, 5)
     ring(1, 4)
+    low2(0)
     low2(1)
+    fixed_part()
     ring(2, 3)
     ring(3, 2)
     first_corner()

time: 86.5 us -> 84.5 us (0.977)
  Pallas kernels: 85.8 us -> 83.4 us
    pallas_call x1, Pallas kernels: 83.1 us -> 80.7 us  [on_device(): pl.pallas_call(kernel, out_shape=(rows, corner, corner, rows, corner), in...]
where the time goes in v4:
time: 84.5 us; the launch traced here: 84 us
  Pallas kernels  83.4 us (99%)
    pallas_call x1, Pallas kernels, on_device(): pl.pallas_call(kernel, out_shape=(rows, corner, corner, rows, corner), in...  80.7 us
    pallas_call x1, Pallas kernels, on_device(): pl.pallas_call(hand_out, out_shape=(rows, corner, corner, rows, corner),...  2.7 us

profile of v4, /device:TPU:8, one launch (start us, length us, event | category | flops | bytes accessed | tf_op | source)
XLA Modules:
  0.0 84.0 jit_solution(14712900113757111725)
XLA Ops:
  0.6 80.7 %inverse.1 = (bf16[128,512]{1,0:T(8,128)(2,1)}, bf16[512,512]{1,0:T(8,128)(2,1)}, bf16[512,512]{1,0:T(8,128)(2,1)}, bf16[128,512]{1,0:T(8,128)(2,1)}, bf16[512,512]{1,0:T(8,128)(2,1)}) custom-call(bf16[16,2048,128]{2,1,0:T(8,128)(2,1)} %bitcast.3, s32[16,16]{1,0:T(8,128)} %bitcast.4, bf16[128,512]{1,0:T(8,128)(2,1)} %p1.1, bf16[128,512]{1,0:T(8,128)(2,1)} %p2.1, ...), custom_call_target="tpu_custom_call" | custom-call | flops 8589934592 | bytes 12582912 | tf_op jit(solution)/shard_map/inverse/pallas_call | solution.py:466
  81.3 2.7 %hand_out.1 = (bf16[128,512]{1,0:T(8,128)(2,1)}, bf16[512,512]{1,0:T(8,128)(2,1)}, bf16[512,512]{1,0:T(8,128)(2,1)}, bf16[128,512]{1,0:T(8,128)(2,1)}, bf16[512,512]{1,0:T(8,128)(2,1)}) custom-call(bf16[128,512]{1,0:T(8,128)(2,1)} %get-tuple-element.10.refs_0_, bf16[512,512]{1,0:T(8,128)(2,1)} %get-tuple-element.11.refs_1_, ...), custom_call_target="tpu_custom_call" | custom-call | tf_op jit(solution)/shard_map/hand_out/pallas_call | solution.py:495
